TPU v7x, 128 devices: a whole 4x4x4 slice. The times are simulated.
128 devices in a mesh: owner: 32 (over y, z, core), group: 4 (over x).
Axes of the slice: x: 4, y: 4, z: 4, core: 2. Of those that a mesh axis runs over, the one named last changes fastest.
Arguments:
- right_side: bfloat16 [64, 2, 4, 4, 128, 128], P('owner', None, 'group'), may hold values from -6 to 6
- hops: bfloat16 [8, 64, 2, 4, 4, 128, 128], P(None, 'owner'), may hold values from -0.09375 to 0.09375
- diag_inverse: bfloat16 [64, 2, 4, 4, 128, 128], P('owner'), may hold values from -0.16 to 2, as said below
- prolongator: bfloat16 [64, 2, 4, 4, 128, 384], P('owner', None, 'group'), may hold values from -0.5 to 0.5
Outputs:
- coarse_solution: bfloat16 [64, 2, 4, 4, 128, 128], P('owner', None, 'group')
- fine_correction: bfloat16 [64, 2, 4, 4, 128, 384], P('owner', None, 'group')
Inputs may be any that keep to these rules, and one draw needn't show every extreme that they name: `diag_inverse`: each site's block has its diagonal entries between 0.25 and 2 and off-diagonal entries of at most 0.16 in magnitude.
All inputs are finite; a program needn't handle non-finite values.
Results may differ from a plain program's by a relative error of at most 0.0067.
Values may be sent and summed in bfloat16 or wider, within the bound.
A program may use at most 128 MiB of HBM per device.

v0:
```python
import jax
import jax.numpy as jnp
from jax import lax
from jax.sharding import PartitionSpec as P

ITERS = 4


def with_halo(cells, sides, width):
    for axis, dim in sides:
        count = lax.axis_size(axis)
        head = lax.slice_in_dim(cells, 0, width, axis=dim)
        tail = lax.slice_in_dim(cells, cells.shape[dim] - width, cells.shape[dim], axis=dim)
        cells = jnp.concatenate(
            [
                lax.ppermute(tail, axis, [(i, (i + 1) % count) for i in range(count)]),
                cells,
                lax.ppermute(head, axis, [((i + 1) % count, i) for i in range(count)]),
            ],
            axis=dim,
        )
    return cells


def hop_total(hops, neighbours):
    total = None
    for direction, neighbour in enumerate(neighbours):
        term = jnp.einsum(
            "tzyxrd,tzyxcd->tzyxrc", neighbour, hops[direction], preferred_element_type=jnp.float32
        )
        total = term if total is None else total + term
    return total


def apply_inverse(inverse, field):
    return jnp.einsum(
        "tzyxcd,tzyxrd->tzyxrc", inverse, field, preferred_element_type=jnp.float32
    ).astype(jnp.bfloat16)


def on_device(right_side, hops, diag_inverse, prolongator):
    slab_width = right_side.shape[2]
    position = lax.axis_index("group")
    gathered = lax.all_gather(right_side, "group", axis=2, tiled=True)
    iterate = apply_inverse(diag_inverse, gathered)
    for iteration in range(ITERS - 1):
        padded = with_halo(iterate, (("owner", 0),), 1)
        neighbours = [
            jnp.roll(iterate, -1, 3),
            jnp.roll(iterate, 1, 3),
            jnp.roll(iterate, -1, 2),
            jnp.roll(iterate, 1, 2),
            jnp.roll(iterate, -1, 1),
            jnp.roll(iterate, 1, 1),
            padded[2:],
            padded[:-2],
        ]
        remainder = (gathered.astype(jnp.float32) - hop_total(hops, neighbours)).astype(
            jnp.bfloat16
        )
        iterate = apply_inverse(diag_inverse, remainder)
    own_part = lax.dynamic_slice_in_dim(iterate, position * slab_width, slab_width, 2)
    fine_correction = jnp.einsum(
        "tzyxrc,tzyxcf->tzyxrf", own_part, prolongator, preferred_element_type=jnp.float32
    ).astype(jnp.bfloat16)
    return (own_part, fine_correction)


def solution(mesh):
    placed = (
        P("owner", None, "group", None, None, None),
        P(None, "owner", None, None, None, None, None),
        P("owner", None, None, None, None, None),
        P("owner", None, "group", None, None, None),
    )
    return jax.shard_map(
        on_device,
        mesh=mesh,
        in_specs=placed,
        out_specs=(
            P("owner", None, "group", None, None, None),
            P("owner", None, "group", None, None, None),
        ),
        check_vma=False,
    )
```

profile of v0, /device:TPU:0, one launch (start us, length us, event | category | flops | bytes accessed | tf_op | source)
XLA Modules:
  0.0 216.7 jit_solution(5484107983098981134)
XLA Ops:
  7.2 0.0 copy-start
  7.2 0.0 all-gather.2.cloned.1.call-start
  7.2 0.7 all-gather.2.cloned.1.call-update
  7.9 35.1 %all-gather.2.cloned.1.call-done = bf16[2,2,4,4,128,128]{5,4,3,2,1,0:T(8,128)(2,1)} async-done(((bf16[2,2,1,4,128,128]{5,4,3,2,1,0:T(8,128)(2,1)}), bf16[2,2,4,4,128,128]{5,4,3,2,1,0:T(8,128)(2,1)}) %all-gather.2.cloned.1.call-update) | async-done | bytes 2097168 | tf_op jit(solution)/shard_map/all_gather | solution.py:44
  43.0 3.3 %convolution_convert_fusion.2 = bf16[2,2,4,4,128,128]{5,4,3,2,1,0:T(8,128)(2,1)S(1)} fusion(bf16[2,2,4,4,128,128]{5,4,3,2,1,0:T(8,128)(2,1)} %all-gather.2.cloned.1.call-done, bf16[2,2,4,4,128,128]{5,4,3,2,1,0:T(8,128)(2,1)S(1)} %copy-done), kind=kOutput, calls=%fused_computation.113 | convolution fusion | flops 269484032 | bytes 6291456 | tf_op jit(solution)/shard_map/tzyxcd,tzyxrd->tzyxrc/dot_general | solution.py:36
  46.3 0.2 fusion.181
  46.5 6.6 %fusion.91 = f32[2,2,4,4,128,128]{5,4,3,2,1,0:T(8,128)} fusion(bf16[8,2,2,4,4,128,128]{6,5,4,3,2,1,0:T(8,128)(2,1)} %param.5, bf16[2,1,4,4,128,128]{5,4,3,2,1,0:T(8,128)(2,1)S(1)} %get-tuple-element.39, bf16[2,1,4,4,128,128]{5,4,3,2,1,0:T(8,128)(2,1)S(1)} %get-tuple-element.38), kind=kOutput, calls=%fused_computation.91 | convolution fusion | flops 269484032 | bytes 8388608 | tf_op jit(solution)/shard_map/tzyxrd,tzyxcd->tzyxrc/dot_general | solution.py:28
  53.1 3.6 %fusion.97 = f32[2,2,4,4,128,128]{5,4,3,2,1,0:T(8,128)} fusion(bf16[8,2,2,4,4,128,128]{6,5,4,3,2,1,0:T(8,128)(2,1)S(1)} %copy-done.4, bf16[2,1,4,4,128,128]{5,4,3,2,1,0:T(8,128)(2,1)S(1)} %get-tuple-element.39, bf16[2,1,4,4,128,128]{5,4,3,2,1,0:T(8,128)(2,1)S(1)} %get-tuple-element.38), kind=kOutput, calls=%fused_computation.97 | convolution fusion | flops 269484032 | bytes 8388608 | tf_op jit(solution)/shard_map/tzyxrd,tzyxcd->tzyxrc/dot_general | solution.py:28
  56.7 0.7 fusion.178
  57.4 0.1 fusion.177
  57.5 0.2 fusion.176
  57.7 4.6 %collective-permute-start = (bf16[1,2,4,4,128,128]{5,4,3,2,1,0:T(8,128)(2,1)S(1)}, bf16[1,2,4,4,128,128]{5,4,3,2,1,0:T(8,128)(2,1)S(1)}, u32[]{:S(2)}, u32[]{:S(2)}) collective-permute-start(bf16[1,2,4,4,128,128]{5,4,3,2,1,0:T(8,128)(2,1)S(1)} %get-tuple-element.29), channel_id=1, source_target_pairs={{4,0},{8,4},{12,8},{16,12},{20,16},{24,20},{28,24},{32,28},{36,32}... | collective-permute-start | bytes 3145736 | tf_op jit(solution)/shard_map/ppermute | solution.py:18
  62.4 0.4 collective-permute-start.1
  62.8 3.6 %fusion.33 = f32[2,2,4,4,128,128]{5,4,3,2,1,0:T(8,128)} fusion(bf16[2,2,4,1,128,128]{5,4,3,2,1,0:T(8,128)(2,1)S(1)} %get-tuple-element.31, bf16[2,2,4,3,128,128]{5,4,3,2,1,0:T(8,128)(2,1)S(1)} %get-tuple-element.33, bf16[8,2,2,4,4,128,128]{6,5,4,3,2,1,0:T(8,128)(2,1)S(1)} %copy-done.4), kind=kOutput, calls=%fused_computation.30 | convolution fusion | flops 269484032 | bytes 8388608 | tf_op jit(solution)/shard_map/tzyxrd,tzyxcd->tzyxrc/dot_general | solution.py:28
  66.4 3.6 %fusion.37 = f32[2,2,4,4,128,128]{5,4,3,2,1,0:T(8,128)} fusion(bf16[2,2,4,3,128,128]{5,4,3,2,1,0:T(8,128)(2,1)S(1)} %get-tuple-element.32, bf16[2,2,4,1,128,128]{5,4,3,2,1,0:T(8,128)(2,1)S(1)} %get-tuple-element.30, bf16[8,2,2,4,4,128,128]{6,5,4,3,2,1,0:T(8,128)(2,1)S(1)} %copy-done.4), kind=kOutput, calls=%fused_computation.34 | convolution fusion | flops 269484032 | bytes 8388608 | tf_op jit(solution)/shard_map/tzyxrd,tzyxcd->tzyxrc/dot_general | solution.py:28
  70.0 0.7 fusion.179
  70.8 0.1 fusion.180
  70.9 3.5 %fusion.41 = f32[2,2,4,4,128,128]{5,4,3,2,1,0:T(8,128)} fusion(bf16[2,2,1,4,128,128]{5,4,3,2,1,0:T(8,128)(2,1)S(1)} %get-tuple-element.36, bf16[2,2,3,4,128,128]{5,4,3,2,1,0:T(8,128)(2,1)S(1)} %get-tuple-element.34, bf16[8,2,2,4,4,128,128]{6,5,4,3,2,1,0:T(8,128)(2,1)S(1)} %copy-done.4), kind=kOutput, calls=%fused_computation.38 | convolution fusion | flops 269484032 | bytes 8388608 | tf_op jit(solution)/shard_map/tzyxrd,tzyxcd->tzyxrc/dot_general | solution.py:28
  74.4 3.5 %fusion.45 = f32[2,2,4,4,128,128]{5,4,3,2,1,0:T(8,128)} fusion(bf16[2,2,3,4,128,128]{5,4,3,2,1,0:T(8,128)(2,1)S(1)} %get-tuple-element.35, bf16[2,2,1,4,128,128]{5,4,3,2,1,0:T(8,128)(2,1)S(1)} %get-tuple-element.37, bf16[8,2,2,4,4,128,128]{6,5,4,3,2,1,0:T(8,128)(2,1)S(1)} %copy-done.4), kind=kOutput, calls=%fused_computation.42 | convolution fusion | flops 269484032 | bytes 8388608 | tf_op jit(solution)/shard_map/tzyxrd,tzyxcd->tzyxrc/dot_general | solution.py:28
  77.9 3.5 %fusion.3 = f32[2,2,4,4,128,128]{5,4,3,2,1,0:T(8,128)} fusion(bf16[1,2,4,4,128,128]{5,4,3,2,1,0:T(8,128)(2,1)S(1)} %collective-permute-done, bf16[2,2,4,4,128,128]{5,4,3,2,1,0:T(8,128)(2,1)S(1)} %convolution_convert_fusion.2, bf16[8,2,2,4,4,128,128]{6,5,4,3,2,1,0:T(8,128)(2,1)S(1)} %copy-done.4), kind=kOutput, calls=%fused_computation.6 | convolution fusion | flops 274726912 | bytes 9437184 | tf_op jit(solution)/shard_map/tzyxrd,tzyxcd->tzyxrc/dot_general | solution.py:28
  81.4 14.4 %fusion = bf16[2,2,4,4,128,128]{5,4,3,2,1,0:T(8,128)(2,1)} fusion(bf16[2,2,4,4,128,128]{5,4,3,2,1,0:T(8,128)(2,1)} %all-gather.2.cloned.1.call-done, f32[2,2,4,4,128,128]{5,4,3,2,1,0:T(8,128)} %fusion.3, f32[2,2,4,4,128,128]{5,4,3,2,1,0:T(8,128)} %fusion.91, f32[2,2,4,4,128,128]{5,4,3,2,1,0:T(8,128)} %fusion.97, f32[2,2,4,4,128,128]{5,4,3,2,1,0:T(8,128)} %fusion.45, ...), kind=kOutput, calls=%fused_computation.3 | convolution fusion | flops 285212672 | bytes 38797312 | tf_op jit(solution)/shard_map/tzyxrd,tzyxcd->tzyxrc/dot_general | solution.py:28
  95.8 3.2 %convolution_convert_fusion.1 = bf16[2,2,4,4,128,128]{5,4,3,2,1,0:T(8,128)(2,1)S(1)} fusion(bf16[2,2,4,4,128,128]{5,4,3,2,1,0:T(8,128)(2,1)} %fusion, bf16[2,2,4,4,128,128]{5,4,3,2,1,0:T(8,128)(2,1)S(1)} %copy-done), kind=kOutput, calls=%fused_computation.112 | convolution fusion | flops 269484032 | bytes 6291456 | tf_op jit(solution)/shard_map/tzyxcd,tzyxrd->tzyxrc/dot_general | solution.py:36
  99.0 0.0 slice-start
  99.0 0.9 fusion.172
  99.9 0.1 fusion.171
  100.1 0.0 slice-start.1
  100.1 0.2 fusion.175
  100.3 0.0 slice-start.2
  100.3 6.0 %fusion.95 = f32[2,2,4,4,128,128]{5,4,3,2,1,0:T(8,128)} fusion(bf16[8,2,2,4,4,128,128]{6,5,4,3,2,1,0:T(8,128)(2,1)} %param.5, bf16[2,1,4,4,128,128]{5,4,3,2,1,0:T(8,128)(2,1)S(1)} %get-tuple-element.27, bf16[2,1,4,4,128,128]{5,4,3,2,1,0:T(8,128)(2,1)S(1)} %get-tuple-element.26), kind=kOutput, calls=%fused_computation.95 | convolution fusion | flops 269484032 | bytes 8388608 | tf_op jit(solution)/shard_map/tzyxrd,tzyxcd->tzyxrc/dot_general | solution.py:28
  106.3 5.3 %fusion.89 = f32[2,2,4,4,128,128]{5,4,3,2,1,0:T(8,128)} fusion(bf16[8,2,2,4,4,128,128]{6,5,4,3,2,1,0:T(8,128)(2,1)} %param.5, bf16[2,1,4,4,128,128]{5,4,3,2,1,0:T(8,128)(2,1)S(1)} %get-tuple-element.27, bf16[2,1,4,4,128,128]{5,4,3,2,1,0:T(8,128)(2,1)S(1)} %get-tuple-element.26), kind=kOutput, calls=%fused_computation.89 | convolution fusion | flops 269484032 | bytes 8388608 | tf_op jit(solution)/shard_map/tzyxrd,tzyxcd->tzyxrc/dot_general | solution.py:28
  111.6 0.2 fusion.170
  111.9 5.1 %collective-permute-start.2 = (bf16[1,2,4,4,128,128]{5,4,3,2,1,0:T(8,128)(2,1)S(1)}, bf16[1,2,4,4,128,128]{5,4,3,2,1,0:T(8,128)(2,1)S(1)}, u32[]{:S(2)}, u32[]{:S(2)}) collective-permute-start(bf16[1,2,4,4,128,128]{5,4,3,2,1,0:T(8,128)(2,1)S(1)} %get-tuple-element.17), channel_id=1, source_target_pairs={{4,0},{8,4},{12,8},{16,12},{20,16},{24,20},{28,24},{32,28},{36,32}... | collective-permute-start | bytes 3145736 | tf_op jit(solution)/shard_map/ppermute | solution.py:18
  117.0 0.2 collective-permute-start.3
  117.2 3.6 %fusion.53 = f32[2,2,4,4,128,128]{5,4,3,2,1,0:T(8,128)} fusion(bf16[2,2,4,3,128,128]{5,4,3,2,1,0:T(8,128)(2,1)S(1)} %get-tuple-element.20, bf16[2,2,4,1,128,128]{5,4,3,2,1,0:T(8,128)(2,1)S(1)} %get-tuple-element.18, bf16[8,2,2,4,4,128,128]{6,5,4,3,2,1,0:T(8,128)(2,1)S(1)} %bitcast.77), kind=kOutput, calls=%fused_computation.51 | convolution fusion | flops 269484032 | bytes 8388608 | tf_op jit(solution)/shard_map/tzyxrd,tzyxcd->tzyxrc/dot_general | solution.py:28
  120.8 3.6 %fusion.49 = f32[2,2,4,4,128,128]{5,4,3,2,1,0:T(8,128)} fusion(bf16[2,2,4,1,128,128]{5,4,3,2,1,0:T(8,128)(2,1)S(1)} %get-tuple-element.19, bf16[2,2,4,3,128,128]{5,4,3,2,1,0:T(8,128)(2,1)S(1)} %get-tuple-element.21, bf16[8,2,2,4,4,128,128]{6,5,4,3,2,1,0:T(8,128)(2,1)S(1)} %bitcast.77), kind=kOutput, calls=%fused_computation.47 | convolution fusion | flops 269484032 | bytes 8388608 | tf_op jit(solution)/shard_map/tzyxrd,tzyxcd->tzyxrc/dot_general | solution.py:28
  124.4 0.7 fusion.173
  125.1 0.1 fusion.174
  125.3 3.5 %fusion.57 = f32[2,2,4,4,128,128]{5,4,3,2,1,0:T(8,128)} fusion(bf16[2,2,1,4,128,128]{5,4,3,2,1,0:T(8,128)(2,1)S(1)} %get-tuple-element.24, bf16[2,2,3,4,128,128]{5,4,3,2,1,0:T(8,128)(2,1)S(1)} %get-tuple-element.22, bf16[8,2,2,4,4,128,128]{6,5,4,3,2,1,0:T(8,128)(2,1)S(1)} %bitcast.77), kind=kOutput, calls=%fused_computation.55 | convolution fusion | flops 269484032 | bytes 8388608 | tf_op jit(solution)/shard_map/tzyxrd,tzyxcd->tzyxrc/dot_general | solution.py:28
  128.8 3.5 %fusion.61 = f32[2,2,4,4,128,128]{5,4,3,2,1,0:T(8,128)} fusion(bf16[2,2,3,4,128,128]{5,4,3,2,1,0:T(8,128)(2,1)S(1)} %get-tuple-element.23, bf16[2,2,1,4,128,128]{5,4,3,2,1,0:T(8,128)(2,1)S(1)} %get-tuple-element.25, bf16[8,2,2,4,4,128,128]{6,5,4,3,2,1,0:T(8,128)(2,1)S(1)} %bitcast.77), kind=kOutput, calls=%fused_computation.59 | convolution fusion | flops 269484032 | bytes 8388608 | tf_op jit(solution)/shard_map/tzyxrd,tzyxcd->tzyxrc/dot_general | solution.py:28
  132.3 3.5 %fusion.11 = f32[2,2,4,4,128,128]{5,4,3,2,1,0:T(8,128)} fusion(bf16[1,2,4,4,128,128]{5,4,3,2,1,0:T(8,128)(2,1)S(1)} %collective-permute-done.2, bf16[2,2,4,4,128,128]{5,4,3,2,1,0:T(8,128)(2,1)S(1)} %convolution_convert_fusion.1, bf16[8,2,2,4,4,128,128]{6,5,4,3,2,1,0:T(8,128)(2,1)S(1)} %bitcast.77), kind=kOutput, calls=%fused_computation.14 | convolution fusion | flops 274726912 | bytes 9437184 | tf_op jit(solution)/shard_map/tzyxrd,tzyxcd->tzyxrc/dot_general | solution.py:28
  135.8 14.4 %fusion.1 = bf16[2,2,4,4,128,128]{5,4,3,2,1,0:T(8,128)(2,1)} fusion(bf16[2,2,4,4,128,128]{5,4,3,2,1,0:T(8,128)(2,1)} %all-gather.2.cloned.1.call-done, f32[2,2,4,4,128,128]{5,4,3,2,1,0:T(8,128)} %fusion.11, f32[2,2,4,4,128,128]{5,4,3,2,1,0:T(8,128)} %fusion.89, f32[2,2,4,4,128,128]{5,4,3,2,1,0:T(8,128)} %fusion.95, f32[2,2,4,4,128,128]{5,4,3,2,1,0:T(8,128)} %fusion.61, ...), kind=kOutput, calls=%fused_computation.4 | convolution fusion | flops 285212672 | bytes 38797312 | tf_op jit(solution)/shard_map/tzyxrd,tzyxcd->tzyxrc/dot_general | solution.py:28
  150.2 3.2 %convolution_convert_fusion = bf16[2,2,4,4,128,128]{5,4,3,2,1,0:T(8,128)(2,1)S(1)} fusion(bf16[2,2,4,4,128,128]{5,4,3,2,1,0:T(8,128)(2,1)} %fusion.1, bf16[2,2,4,4,128,128]{5,4,3,2,1,0:T(8,128)(2,1)S(1)} %copy-done), kind=kOutput, calls=%fused_computation.111 | convolution fusion | flops 269484032 | bytes 6291456 | tf_op jit(solution)/shard_map/tzyxcd,tzyxrd->tzyxrc/dot_general | solution.py:36
  153.4 0.0 slice-start.4
  153.4 0.9 fusion.166
  154.3 0.1 fusion.165
  154.4 0.0 slice-start.5
  154.4 0.2 fusion.169
  154.6 0.0 slice-start.6
  154.6 6.0 %fusion.93 = f32[2,2,4,4,128,128]{5,4,3,2,1,0:T(8,128)} fusion(bf16[8,2,2,4,4,128,128]{6,5,4,3,2,1,0:T(8,128)(2,1)} %param.5, bf16[2,1,4,4,128,128]{5,4,3,2,1,0:T(8,128)(2,1)S(1)} %get-tuple-element.15, bf16[2,1,4,4,128,128]{5,4,3,2,1,0:T(8,128)(2,1)S(1)} %get-tuple-element.14), kind=kOutput, calls=%fused_computation.93 | convolution fusion | flops 269484032 | bytes 8388608 | tf_op jit(solution)/shard_map/tzyxrd,tzyxcd->tzyxrc/dot_general | solution.py:28
  160.7 5.3 %fusion.87 = f32[2,2,4,4,128,128]{5,4,3,2,1,0:T(8,128)} fusion(bf16[8,2,2,4,4,128,128]{6,5,4,3,2,1,0:T(8,128)(2,1)} %param.5, bf16[2,1,4,4,128,128]{5,4,3,2,1,0:T(8,128)(2,1)S(1)} %get-tuple-element.15, bf16[2,1,4,4,128,128]{5,4,3,2,1,0:T(8,128)(2,1)S(1)} %get-tuple-element.14), kind=kOutput, calls=%fused_computation.87 | convolution fusion | flops 269484032 | bytes 8388608 | tf_op jit(solution)/shard_map/tzyxrd,tzyxcd->tzyxrc/dot_general | solution.py:28
  166.0 0.2 fusion.164
  166.2 5.1 %collective-permute-start.4 = (bf16[1,2,4,4,128,128]{5,4,3,2,1,0:T(8,128)(2,1)S(1)}, bf16[1,2,4,4,128,128]{5,4,3,2,1,0:T(8,128)(2,1)S(1)}, u32[]{:S(2)}, u32[]{:S(2)}) collective-permute-start(bf16[1,2,4,4,128,128]{5,4,3,2,1,0:T(8,128)(2,1)S(1)} %get-tuple-element.5), channel_id=1, source_target_pairs={{4,0},{8,4},{12,8},{16,12},{20,16},{24,20},{28,24},{32,28},{36,32}... | collective-permute-start | bytes 3145736 | tf_op jit(solution)/shard_map/ppermute | solution.py:18
  171.3 0.2 collective-permute-start.5
  171.6 3.6 %fusion.69 = f32[2,2,4,4,128,128]{5,4,3,2,1,0:T(8,128)} fusion(bf16[2,2,4,3,128,128]{5,4,3,2,1,0:T(8,128)(2,1)S(1)} %get-tuple-element.8, bf16[2,2,4,1,128,128]{5,4,3,2,1,0:T(8,128)(2,1)S(1)} %get-tuple-element.6, bf16[8,2,2,4,4,128,128]{6,5,4,3,2,1,0:T(8,128)(2,1)S(1)} %bitcast.79), kind=kOutput, calls=%fused_computation.68 | convolution fusion | flops 269484032 | bytes 8388608 | tf_op jit(solution)/shard_map/tzyxrd,tzyxcd->tzyxrc/dot_general | solution.py:28
  175.2 3.6 %fusion.65 = f32[2,2,4,4,128,128]{5,4,3,2,1,0:T(8,128)} fusion(bf16[2,2,4,1,128,128]{5,4,3,2,1,0:T(8,128)(2,1)S(1)} %get-tuple-element.7, bf16[2,2,4,3,128,128]{5,4,3,2,1,0:T(8,128)(2,1)S(1)} %get-tuple-element.9, bf16[8,2,2,4,4,128,128]{6,5,4,3,2,1,0:T(8,128)(2,1)S(1)} %bitcast.79), kind=kOutput, calls=%fused_computation.64 | convolution fusion | flops 269484032 | bytes 8388608 | tf_op jit(solution)/shard_map/tzyxrd,tzyxcd->tzyxrc/dot_general | solution.py:28
  178.8 0.7 fusion.167
  179.5 0.1 fusion.168
  179.6 3.5 %fusion.73 = f32[2,2,4,4,128,128]{5,4,3,2,1,0:T(8,128)} fusion(bf16[2,2,1,4,128,128]{5,4,3,2,1,0:T(8,128)(2,1)S(1)} %get-tuple-element.12, bf16[2,2,3,4,128,128]{5,4,3,2,1,0:T(8,128)(2,1)S(1)} %get-tuple-element.10, bf16[8,2,2,4,4,128,128]{6,5,4,3,2,1,0:T(8,128)(2,1)S(1)} %bitcast.79), kind=kOutput, calls=%fused_computation.72 | convolution fusion | flops 269484032 | bytes 8388608 | tf_op jit(solution)/shard_map/tzyxrd,tzyxcd->tzyxrc/dot_general | solution.py:28
  183.1 3.5 %fusion.77 = f32[2,2,4,4,128,128]{5,4,3,2,1,0:T(8,128)} fusion(bf16[2,2,3,4,128,128]{5,4,3,2,1,0:T(8,128)(2,1)S(1)} %get-tuple-element.11, bf16[2,2,1,4,128,128]{5,4,3,2,1,0:T(8,128)(2,1)S(1)} %get-tuple-element.13, bf16[8,2,2,4,4,128,128]{6,5,4,3,2,1,0:T(8,128)(2,1)S(1)} %bitcast.79), kind=kOutput, calls=%fused_computation.76 | convolution fusion | flops 269484032 | bytes 8388608 | tf_op jit(solution)/shard_map/tzyxrd,tzyxcd->tzyxrc/dot_general | solution.py:28
  186.6 3.5 %fusion.19 = f32[2,2,4,4,128,128]{5,4,3,2,1,0:T(8,128)} fusion(bf16[1,2,4,4,128,128]{5,4,3,2,1,0:T(8,128)(2,1)S(1)} %collective-permute-done.4, bf16[2,2,4,4,128,128]{5,4,3,2,1,0:T(8,128)(2,1)S(1)} %convolution_convert_fusion, bf16[8,2,2,4,4,128,128]{6,5,4,3,2,1,0:T(8,128)(2,1)S(1)} %bitcast.79), kind=kOutput, calls=%fused_computation.22 | convolution fusion | flops 274726912 | bytes 9437184 | tf_op jit(solution)/shard_map/tzyxrd,tzyxcd->tzyxrc/dot_general | solution.py:28
  190.1 14.4 %fusion.2 = bf16[2,2,4,4,128,128]{5,4,3,2,1,0:T(8,128)(2,1)} fusion(bf16[2,2,4,4,128,128]{5,4,3,2,1,0:T(8,128)(2,1)} %all-gather.2.cloned.1.call-done, f32[2,2,4,4,128,128]{5,4,3,2,1,0:T(8,128)} %fusion.19, f32[2,2,4,4,128,128]{5,4,3,2,1,0:T(8,128)} %fusion.87, f32[2,2,4,4,128,128]{5,4,3,2,1,0:T(8,128)} %fusion.93, f32[2,2,4,4,128,128]{5,4,3,2,1,0:T(8,128)} %fusion.77, ...), kind=kOutput, calls=%fused_computation.5 | convolution fusion | flops 285212672 | bytes 38797312 | tf_op jit(solution)/shard_map/tzyxrd,tzyxcd->tzyxrc/dot_general | solution.py:28
  204.5 3.3 %fusion.182 = bf16[2,2,4,4,128,128]{5,4,3,2,1,0:T(8,128)(2,1)S(1)} fusion(bf16[2,2,4,4,128,128]{5,4,3,2,1,0:T(8,128)(2,1)} %fusion.2, bf16[2,2,4,4,128,128]{5,4,3,2,1,0:T(8,128)(2,1)S(1)} %copy-done), kind=kOutput, calls=%fused_computation.185 | convolution fusion | flops 268435456 | bytes 6291456 | tf_op jit(solution)/shard_map/tzyxcd,tzyxrd->tzyxrc/dot_general | solution.py:36
  207.9 0.0 copy-start.5
  207.9 1.7 fusion.136
  (31 shorter events, 0.1 us)
Async XLA Ops:
  7.2 35.8 %copy-start = (bf16[2,2,4,4,128,128]{5,4,3,2,1,0:T(8,128)(2,1)S(1)}, bf16[2,2,4,4,128,128]{5,4,3,2,1,0:T(8,128)(2,1)}, u32[]{:S(2)}) copy-start(bf16[2,2,4,4,128,128]{5,4,3,2,1,0:T(8,128)(2,1)} %param.6) | copy-start | bytes 6291460
  7.2 35.8 %all-gather.2.cloned.1.call-start = ((), (), s32[]{:S(2)}) async-start(), calls=%async_computation | async-start | bytes 2621440 | tf_op jit(solution)/shard_map/all_gather | solution.py:44
  43.0 10.1 %copy-start.4 = (bf16[8,2,2,4,4,128,128]{6,5,4,3,2,1,0:T(8,128)(2,1)S(1)}, bf16[8,2,2,4,4,128,128]{6,5,4,3,2,1,0:T(8,128)(2,1)}, u32[]{:S(2)}) copy-start(bf16[8,2,2,4,4,128,128]{6,5,4,3,2,1,0:T(8,128)(2,1)} %param.5) | copy-start | bytes 50331652
  46.3 31.6 %copy-start.3 = (bf16[2,2,4,4,128,128]{5,4,3,2,1,0:T(8,128)(2,1)}, bf16[2,2,4,4,128,128]{5,4,3,2,1,0:T(8,128)(2,1)S(1)}, u32[]{:S(2)}) copy-start(bf16[2,2,4,4,128,128]{5,4,3,2,1,0:T(8,128)(2,1)S(1)} %convolution_convert_fusion.2) | copy-start | bytes 6291460
  57.7 20.2 %collective-permute-start = (bf16[1,2,4,4,128,128]{5,4,3,2,1,0:T(8,128)(2,1)S(1)}, bf16[1,2,4,4,128,128]{5,4,3,2,1,0:T(8,128)(2,1)S(1)}, u32[]{:S(2)}, u32[]{:S(2)}) collective-permute-start(bf16[1,2,4,4,128,128]{5,4,3,2,1,0:T(8,128)(2,1)S(1)} %get-tuple-element.29), channel_id=1, source_target_pairs={{4,0},{8,4},{12,8},{16,12},{20,16},{24,20},{28,24},{32,28},{36,32}... | collective-permute-start | bytes 3145736 | tf_op jit(solution)/shard_map/ppermute | solution.py:18
  62.4 19.0 %collective-permute-start.1 = (bf16[1,2,4,4,128,128]{5,4,3,2,1,0:T(8,128)(2,1)S(1)}, bf16[1,2,4,4,128,128]{5,4,3,2,1,0:T(8,128)(2,1)S(1)}, u32[]{:S(2)}, u32[]{:S(2)}) collective-permute-start(bf16[1,2,4,4,128,128]{5,4,3,2,1,0:T(8,128)(2,1)S(1)} %get-tuple-element.28), channel_id=1, source_target_pairs={{0,4},{4,8},{8,12},{12,16},{16,20},{20,24},{24,28},{28,32},{32,36}... | collective-permute-start | bytes 3145736 | tf_op jit(solution)/shard_map/ppermute | solution.py:16
  99.0 33.3 %copy-start.2 = (bf16[2,2,4,4,128,128]{5,4,3,2,1,0:T(8,128)(2,1)}, bf16[2,2,4,4,128,128]{5,4,3,2,1,0:T(8,128)(2,1)S(1)}, u32[]{:S(2)}) copy-start(bf16[2,2,4,4,128,128]{5,4,3,2,1,0:T(8,128)(2,1)S(1)} %convolution_convert_fusion.1) | copy-start | bytes 6291460
  99.0 18.2 %slice-start = ((s8[16777216]{0:T(1024)(128)(4,1)}), s8[4194304]{0:T(1024)(128)(4,1)S(1)}, s32[]{:S(2)}) async-start(s8[16777216]{0:T(1024)(128)(4,1)} %bitcast.76), calls=%async_computation.1 | async-start | bytes 8388608
  100.1 17.1 %slice-start.1 = ((s8[16777216]{0:T(1024)(128)(4,1)}), s8[4194304]{0:T(1024)(128)(4,1)S(1)}, s32[]{:S(2)}) async-start(s8[16777216]{0:T(1024)(128)(4,1)} %bitcast.76), calls=%async_computation.2 | async-start | bytes 8388608
  100.3 16.9 %slice-start.2 = ((s8[16777216]{0:T(1024)(128)(4,1)}), s8[4194304]{0:T(1024)(128)(4,1)S(1)}, s32[]{:S(2)}) async-start(s8[16777216]{0:T(1024)(128)(4,1)} %bitcast.76), calls=%async_computation.3 | async-start | bytes 8388608
  106.3 10.9 %slice-start.3 = ((s8[16777216]{0:T(1024)(128)(4,1)}), s8[4194304]{0:T(1024)(128)(4,1)S(1)}, s32[]{:S(2)}) async-start(s8[16777216]{0:T(1024)(128)(4,1)} %bitcast.76), calls=%async_computation.4 | async-start | bytes 8388608
  111.9 20.4 %collective-permute-start.2 = (bf16[1,2,4,4,128,128]{5,4,3,2,1,0:T(8,128)(2,1)S(1)}, bf16[1,2,4,4,128,128]{5,4,3,2,1,0:T(8,128)(2,1)S(1)}, u32[]{:S(2)}, u32[]{:S(2)}) collective-permute-start(bf16[1,2,4,4,128,128]{5,4,3,2,1,0:T(8,128)(2,1)S(1)} %get-tuple-element.17), channel_id=1, source_target_pairs={{4,0},{8,4},{12,8},{16,12},{20,16},{24,20},{28,24},{32,28},{36,32}... | collective-permute-start | bytes 3145736 | tf_op jit(solution)/shard_map/ppermute | solution.py:18
  117.0 18.8 %collective-permute-start.3 = (bf16[1,2,4,4,128,128]{5,4,3,2,1,0:T(8,128)(2,1)S(1)}, bf16[1,2,4,4,128,128]{5,4,3,2,1,0:T(8,128)(2,1)S(1)}, u32[]{:S(2)}, u32[]{:S(2)}) collective-permute-start(bf16[1,2,4,4,128,128]{5,4,3,2,1,0:T(8,128)(2,1)S(1)} %get-tuple-element.16), channel_id=1, source_target_pairs={{0,4},{4,8},{8,12},{12,16},{16,20},{20,24},{24,28},{28,32},{32,36}... | collective-permute-start | bytes 3145736 | tf_op jit(solution)/shard_map/ppermute | solution.py:16
  153.4 33.3 %copy-start.1 = (bf16[2,2,4,4,128,128]{5,4,3,2,1,0:T(8,128)(2,1)}, bf16[2,2,4,4,128,128]{5,4,3,2,1,0:T(8,128)(2,1)S(1)}, u32[]{:S(2)}) copy-start(bf16[2,2,4,4,128,128]{5,4,3,2,1,0:T(8,128)(2,1)S(1)} %convolution_convert_fusion) | copy-start | bytes 6291460
  153.4 18.1 %slice-start.4 = ((s8[16777216]{0:T(1024)(128)(4,1)}), s8[4194304]{0:T(1024)(128)(4,1)S(1)}, s32[]{:S(2)}) async-start(s8[16777216]{0:T(1024)(128)(4,1)} %bitcast.78), calls=%async_computation.5 | async-start | bytes 8388608
  154.4 17.1 %slice-start.5 = ((s8[16777216]{0:T(1024)(128)(4,1)}), s8[4194304]{0:T(1024)(128)(4,1)S(1)}, s32[]{:S(2)}) async-start(s8[16777216]{0:T(1024)(128)(4,1)} %bitcast.78), calls=%async_computation.6 | async-start | bytes 8388608
  154.6 16.9 %slice-start.6 = ((s8[16777216]{0:T(1024)(128)(4,1)}), s8[4194304]{0:T(1024)(128)(4,1)S(1)}, s32[]{:S(2)}) async-start(s8[16777216]{0:T(1024)(128)(4,1)} %bitcast.78), calls=%async_computation.7 | async-start | bytes 8388608
  160.7 10.9 %slice-start.7 = ((s8[16777216]{0:T(1024)(128)(4,1)}), s8[4194304]{0:T(1024)(128)(4,1)S(1)}, s32[]{:S(2)}) async-start(s8[16777216]{0:T(1024)(128)(4,1)} %bitcast.78), calls=%async_computation.8 | async-start | bytes 8388608
  166.2 20.4 %collective-permute-start.4 = (bf16[1,2,4,4,128,128]{5,4,3,2,1,0:T(8,128)(2,1)S(1)}, bf16[1,2,4,4,128,128]{5,4,3,2,1,0:T(8,128)(2,1)S(1)}, u32[]{:S(2)}, u32[]{:S(2)}) collective-permute-start(bf16[1,2,4,4,128,128]{5,4,3,2,1,0:T(8,128)(2,1)S(1)} %get-tuple-element.5), channel_id=1, source_target_pairs={{4,0},{8,4},{12,8},{16,12},{20,16},{24,20},{28,24},{32,28},{36,32}... | collective-permute-start | bytes 3145736 | tf_op jit(solution)/shard_map/ppermute | solution.py:18
  171.3 18.8 %collective-permute-start.5 = (bf16[1,2,4,4,128,128]{5,4,3,2,1,0:T(8,128)(2,1)S(1)}, bf16[1,2,4,4,128,128]{5,4,3,2,1,0:T(8,128)(2,1)S(1)}, u32[]{:S(2)}, u32[]{:S(2)}) collective-permute-start(bf16[1,2,4,4,128,128]{5,4,3,2,1,0:T(8,128)(2,1)S(1)} %get-tuple-element.4), channel_id=1, source_target_pairs={{0,4},{4,8},{8,12},{12,16},{16,20},{20,24},{24,28},{28,32},{32,36}... | collective-permute-start | bytes 3145736 | tf_op jit(solution)/shard_map/ppermute | solution.py:16
  204.5 3.3 %copy-start.6 = (bf16[2,2,1,4,128,384]{5,4,3,2,1,0:T(8,128)(2,1)S(1)}, bf16[2,2,1,4,128,384]{5,4,3,2,1,0:T(8,128)(2,1)}, u32[]{:S(2)}) copy-start(bf16[2,2,1,4,128,384]{5,4,3,2,1,0:T(8,128)(2,1)} %param.7) | copy-start | bytes 4718596
  207.9 1.7 copy-start.5
Sparse Core Ops, SparseCore 0:
  9.7 33.2 all-gather.1
where the time goes:
time: 221 us; the launch traced here: 217 us
  matrix products  144 us (65%)
  waiting for transfers between devices  35.8 us (16%)
  starting transfers between devices  15.7 us (7%)
  between operations  14.6 us (7%)
  local copies, waits for them, and re-layouts  6.74 us (3%)
    dot_general x24, matrix products, hop_total(): jnp.einsum('tzyxrd,tzyxcd->tzyxrc', neighbour, hops[direction], preferred...  129 us
    all_gather x1, waiting for transfers between devices, on_device(): gathered = lax.all_gather(right_side, 'group', axis=2, tiled=True)  35.1 us
    ppermute x3, starting transfers between devices, with_halo(): lax.ppermute(head, axis, [((i + 1) % count, i) for i in range(count)])  14.8 us
    dot_general x4, matrix products, apply_inverse(): jnp.einsum('tzyxcd,tzyxrd->tzyxrc', inverse, field, preferred_element_typ...  12.9 us
  transfers between devices with their start and end apart: 7, of which 1 were waited for; matrix products, arithmetic and copies ran while one was open for 26% of the time, Pallas kernels for 0%

commit v1 on v0

v1 whole, which is shorter than its diff:
```python
import functools

import jax
import jax.numpy as jnp
from jax import lax
from jax.experimental import pallas as pl
from jax.experimental.pallas import tpu as pltpu
from jax.sharding import PartitionSpec as P

MESH = pl.DeviceIdType.MESH
ITERS = 4
C = 128
PART = 32
DIRS = 7
F32 = jnp.float32
BF16 = jnp.bfloat16


def dot(left, right):
    return lax.dot_general(
        left, right, (((1,), (0,)), ((), ())), preferred_element_type=F32
    )


def ring(step):
    return step + step // 2 - 2 * (step // 3)


def ring_of(step):
    return step + lax.div(step, 2) - 2 * lax.div(step, 3)


def kernel(
    b_hbm, h_hbm, d_hbm, p_hbm, c_hbm, f_hbm,
    hs, ht, ds, rhs, field, last, acc, gathered, pro, fine,
    h_sem, d_sem, p_sem, b_sem, c_sem, f_sem,
    in_send, in_recv, halo_send, halo_recv, out_send, out_recv,
):
    g = lax.axis_index("group")
    o = lax.axis_index("owner")
    before, after = lax.rem(o + 31, 32), lax.rem(o + 1, 32)

    def slab(j):
        return lax.rem(g + ring_of(j), 4)

    def part(index):
        return pl.ds(pl.multiple_of(index * PART, PART), PART)

    d_load = pltpu.make_async_copy(d_hbm, ds, d_sem)
    d_load.start()
    b_load = pltpu.make_async_copy(b_hbm.at[:, :, 0, :, part(g), :], rhs.at[:, :, g], b_sem)
    b_load.start()

    def h_load(j, t, z):
        y = slab(j)
        return pltpu.make_async_copy(
            h_hbm.at[:, t, z, y], hs.at[:, t, z, y], h_sem.at[j, t, z]
        )

    def start_loads(j, carry):
        for t in range(2):
            for z in range(2):
                h_load(j, t, z).start()
        return carry

    lax.fori_loop(0, 4, start_loads, 0)
    p_load = pltpu.make_async_copy(p_hbm.at[:, :, 0], pro, p_sem)
    p_load.start()

    barrier = pltpu.get_barrier_semaphore()
    for k in (1, 2, 3):
        pl.semaphore_signal(
            barrier, inc=1, device_id={"group": lax.rem(g + k, 4)}, device_id_type=MESH
        )
    for neighbour in (before, after):
        pl.semaphore_signal(
            barrier, inc=1, device_id={"owner": neighbour}, device_id_type=MESH
        )
    pl.semaphore_wait(barrier, 5)

    opposite = {1: 2, 2: 1, 3: 3}

    def in_copy(j):
        peer = lax.rem(g + ring(j), 4)
        return pltpu.make_async_remote_copy(
            src_ref=b_hbm.at[:, :, 0, :, part(peer), :],
            dst_ref=rhs.at[:, :, g],
            send_sem=in_send.at[j],
            recv_sem=in_recv.at[opposite[j]],
            device_id={"group": peer},
            device_id_type=MESH,
        )

    def in_arrival(j):
        peer = lax.rem(g + ring(j), 4)
        return pltpu.make_async_remote_copy(
            src_ref=b_hbm.at[:, :, 0, :, part(peer), :],
            dst_ref=rhs.at[:, :, peer],
            send_sem=in_send.at[j],
            recv_sem=in_recv.at[j],
            device_id={"group": peer},
            device_id_type=MESH,
        )

    for j in (3, 1, 2):
        in_copy(j).start()

    def halo_copy(it, j, side):
        y = slab(j)
        return pltpu.make_async_remote_copy(
            src_ref=field.at[it, 2 - side, :, y],
            dst_ref=field.at[it, 3 * side, :, y],
            send_sem=halo_send.at[it, j, side],
            recv_sem=halo_recv.at[it, j, side],
            device_id={"owner": before if side else after},
            device_id_type=MESH,
        )

    def send_halo(it, j):
        for side in range(2):
            halo_copy(it, j, side).start()

    def wait_halo(it, j):
        for side in range(2):
            halo_copy(it, j, side).wait_recv()

    sites = [(t, z, x) for t in range(2) for z in range(2) for x in range(4)]

    def transpose_slab(j, carry):
        y = slab(j)
        for t in range(2):
            for z in range(2):
                h_load(j, t, z).wait()
                for x in range(4):
                    inner, outer = (6, 7) if t == 0 else (7, 6)
                    blocks = [hs[k, t, z, y, x] for k in range(4)]
                    blocks.append(hs[4, t, z, y, x] + hs[5, t, z, y, x])
                    blocks.append(hs[inner, t, z, y, x])
                    blocks.append(hs[outer, t, z, y, x])
                    for k, block in enumerate(blocks):
                        ht[t, z, y, x, k * C : (k + 1) * C, :] = block.T
                    ds[t, z, y, x] = ds[t, z, y, x].T
        return carry

    def first(j):
        y = slab(j)
        for t, z, x in sites:
            field[0, t + 1, z, y, x] = dot(rhs[t, z, y, x], ds[t, z, y, x]).astype(BF16)
        send_halo(0, j)

    def interior(it, j):
        y = slab(j)
        up, down = lax.rem(y + 1, 4), lax.rem(y + 3, 4)
        for q, (t, z, x) in enumerate(sites):
            near = jnp.concatenate(
                [
                    field[it, t + 1, z, y, (x + 1) % 4],
                    field[it, t + 1, z, y, (x + 3) % 4],
                    field[it, t + 1, z, up, x],
                    field[it, t + 1, z, down, x],
                    field[it, t + 1, 1 - z, y, x],
                    field[it, 2 - t, z, y, x],
                ],
                axis=1,
            )
            total = dot(near, ht[t, z, y, x, : 6 * C, :])
            acc[q] = rhs[t, z, y, x].astype(F32) - total

    def finish(it, j, store):
        y = slab(j)
        remainders = [
            (acc[q] - dot(field[it, 3 * t, z, y, x], ht[t, z, y, x, 6 * C :, :])).astype(BF16)
            for q, (t, z, x) in enumerate(sites)
        ]
        for remainder, (t, z, x) in zip(remainders, sites):
            store(t, z, y, x, dot(remainder, ds[t, z, y, x]).astype(BF16))

    d_load.wait()
    transpose_slab(0, 0)
    b_load.wait()
    first(0)
    lax.fori_loop(1, 4, transpose_slab, 0)
    for j in range(1, 4):
        in_arrival(j).wait_recv()
        first(j)

    interior(0, 0)
    for it in range(ITERS - 2):

        def store(t, z, y, x, value, it=it):
            field[it + 1, t + 1, z, y, x] = value

        def step(j, carry, it=it, store=store):
            wait_halo(it, j)
            finish(it, j, store)
            send_halo(it + 1, j)
            lax.cond(j < 3, lambda: interior(it, j + 1), lambda: interior(it + 1, 0))
            return carry

        lax.fori_loop(0, 4, step, 0)

    def out_copy(j):
        peer = slab(j)
        return pltpu.make_async_remote_copy(
            src_ref=last.at[:, :, peer],
            dst_ref=gathered.at[:, :, :, part(g), :],
            send_sem=out_send.at[j],
            recv_sem=out_recv.at[j],
            device_id={"group": peer},
            device_id_type=MESH,
        )

    def store_last(t, z, y, x, value):
        last[t, z, y, x] = value

    def store_own(t, z, y, x, value):
        gathered[t, z, x, part(g), :] = value

    it = ITERS - 2
    wait_halo(it, 0)
    finish(it, 0, store_own)

    def last_step(j, carry):
        interior(it, j)
        wait_halo(it, j)
        finish(it, j, store_last)
        out_copy(j).start()
        return carry

    lax.fori_loop(1, 4, last_step, 0)

    p_load.wait()
    for j in range(1, 4):
        out_copy(j).wait_recv()
    c_store = pltpu.make_async_copy(gathered, c_hbm.at[:, :, 0], c_sem)
    c_store.start()

    def f_store(t, z):
        return pltpu.make_async_copy(fine.at[t, z], f_hbm.at[t, z, 0], f_sem.at[t, z])

    for t in range(2):
        for z in range(2):
            for x in range(4):
                fine[t, z, x] = dot(gathered[t, z, x], pro[t, z, x]).astype(BF16)
            f_store(t, z).start()

    c_store.wait()
    for t in range(2):
        for z in range(2):
            f_store(t, z).wait()
    for j in range(1, 4):
        in_copy(j).wait_send()
        out_copy(j).wait_send()

    def drain(j, carry):
        for k in range(ITERS - 1):
            for side in range(2):
                halo_copy(k, j, side).wait_send()
        return carry

    lax.fori_loop(0, 4, drain, 0)


def on_device(right_side, hops, diag_inverse, prolongator):
    vmem, dma = pltpu.VMEM, pltpu.SemaphoreType.DMA
    fine_width = prolongator.shape[-1]
    return pl.pallas_call(
        kernel,
        out_shape=(
            jax.ShapeDtypeStruct(right_side.shape, BF16),
            jax.ShapeDtypeStruct(prolongator.shape, BF16),
        ),
        in_specs=[pl.BlockSpec(memory_space=pl.ANY)] * 4,
        out_specs=(pl.BlockSpec(memory_space=pl.ANY),) * 2,
        scratch_shapes=[
            vmem((8, 2, 2, 4, 4, C, C), BF16),
            vmem((2, 2, 4, 4, DIRS * C, C), BF16),
            vmem((2, 2, 4, 4, C, C), BF16),
            vmem((2, 2, 4, 4, PART, C), BF16),
            vmem((ITERS - 1, 4, 2, 4, 4, PART, C), BF16),
            vmem((2, 2, 4, 4, PART, C), BF16),
            vmem((16, PART, C), F32),
            vmem((2, 2, 4, C, C), BF16),
            vmem((2, 2, 4, C, fine_width), BF16),
            vmem((2, 2, 4, C, fine_width), BF16),
            dma((4, 2, 2)),
            dma,
            dma,
            dma,
            dma,
            dma((2, 2)),
            dma((4,)),
            dma((4,)),
            dma((ITERS - 1, 4, 2)),
            dma((ITERS - 1, 4, 2)),
            dma((4,)),
            dma((4,)),
        ],
        compiler_params=pltpu.CompilerParams(
            collective_id=0, has_side_effects=True, vmem_limit_bytes=60 * 1024 * 1024
        ),
        cost_estimate=pl.CostEstimate(
            flops=2 * 64 * 28 * C * C * PART, bytes_accessed=24 * 1024 * 1024, transcendentals=0
        ),
    )(right_side, hops, diag_inverse, prolongator)


def solution(mesh):
    placed = (
        P("owner", None, "group", None, None, None),
        P(None, "owner", None, None, None, None, None),
        P("owner", None, None, None, None, None),
        P("owner", None, "group", None, None, None),
    )
    return jax.shard_map(
        on_device,
        mesh=mesh,
        in_specs=placed,
        out_specs=(
            P("owner", None, "group", None, None, None),
            P("owner", None, "group", None, None, None),
        ),
        check_vma=False,
    )
```

time: 221 us -> 43.5 us (0.20); the launches traced: 217 us -> 43 us
  matrix products: 144 us -> 0 us
  Pallas kernels: 0 us -> 37.8 us
  waiting for transfers between devices: 35.8 us -> 0 us
  starting transfers between devices: 15.7 us -> 0 us
  between operations: 14.6 us -> 0.64 us
    dot_general x29 -> x0, matrix products: 144 us -> none  [the longest x24 129 us: hop_total(): jnp.einsum('tzyxrd,tzyxcd->tzyxrc', neighbour, hops[direction], preferred...]
    pallas_call x0 -> x1, Pallas kernels: none -> 37.8 us  [on_device(): pl.pallas_call(kernel, out_shape=(jax.ShapeDtypeStruct(right_side.shape,...]
    all_gather x1 -> x0, waiting for transfers between devices: 35.1 us -> none  [on_device(): gathered = lax.all_gather(right_side, 'group', axis=2, tiled=True)]
    ppermute x6 -> x0, starting transfers between devices: 15.6 us -> none  [the longest x3 14.8 us: with_halo(): lax.ppermute(head, axis, [((i + 1) % count, i) for i in range(count)])]
    slice x18 -> x0, local copies, waits for them, and re-layouts: 6.61 us -> none  [the longest x6 2.87 us: on_device(): jnp.roll(iterate, 1, 3)]
    unnamed x30 -> x2, local copies, waits for them, and re-layouts: 0.09 us -> 4.64 us
  transfers between devices with their start and end apart: 7 -> 0, of which waited for: 1 -> 0; matrix products, arithmetic and copies ran while one was open for 26% -> 0% of each run, Pallas kernels for 0% -> 0%
where the time goes in v1:
time: 43.5 us; the launch traced here: 43 us
  Pallas kernels  37.8 us (87%)
  local copies, waits for them, and re-layouts  4.64 us (11%)
  between operations  0.64 us (1%)
    pallas_call x1, Pallas kernels, on_device(): pl.pallas_call(kernel, out_shape=(jax.ShapeDtypeStruct(right_side.shape,...  37.8 us
    unnamed x2, local copies, waits for them, and re-layouts  4.64 us

profile of v1, /device:TPU:0, one launch (start us, length us, event | category | flops | bytes accessed | tf_op | source)
XLA Modules:
  0.0 43.0 jit_solution(1544960230991641792)
XLA Ops:
  0.6 37.8 %shard_map.59 = (bf16[2,2,1,4,128,128]{5,4,3,2,1,0:T(8,128)(2,1)}, bf16[2,2,1,4,128,384]{5,4,3,2,1,0:T(8,128)(2,1)}) custom-call(bf16[2,2,1,4,128,128]{5,4,3,2,1,0:T(8,128)(2,1)} %b_hbm.1, bf16[8,2,2,4,4,128,128]{6,5,4,3,2,1,0:T(8,128)(2,1)} %h_hbm.1, bf16[2,2,4,4,128,128]{5,4,3,2,1,0:T(8,128)(2,1)} %d_hbm.1, bf16[2,2,1,4,128,384]{5,4,3,2,1,0:T(8,128)(2,1)} %p_hbm.1), custom_call_target="tpu_custom_call" | custom-call | flops 1879048192 | bytes 25165824 | tf_op jit(solution)/shard_map/pallas_call | solution.py:267
  38.4 1.9 %copy.8 = bf16[2,2,1,4,128,128]{5,4,3,2,1,0:T(8,128)(2,1)} copy(bf16[2,2,1,4,128,128]{5,4,3,2,1,0:T(8,128)(2,1)} %get-tuple-element.4) | data formatting | bytes 1048576
  40.3 2.8 %copy.9 = bf16[2,2,1,4,128,384]{5,4,3,2,1,0:T(8,128)(2,1)} copy(bf16[2,2,1,4,128,384]{5,4,3,2,1,0:T(8,128)(2,1)} %get-tuple-element.5) | data formatting | bytes 3145728

commit v2 on v0

v2 whole, which is shorter than its diff:
```python
import functools

import jax
import jax.numpy as jnp
from jax import lax
from jax.experimental import pallas as pl
from jax.experimental.pallas import tpu as pltpu
from jax.sharding import PartitionSpec as P

MESH = pl.DeviceIdType.MESH
ITERS = 4
C = 128
PART = 32
DIRS = 7
OFF, IN = 0, 1
VMEM_LIMIT = 56 * 1024 * 1024
F32 = jnp.float32
BF16 = jnp.bfloat16


def dot(left, right):
    return lax.dot_general(
        left, right, (((1,), (0,)), ((), ())), preferred_element_type=F32
    )


def offset_of(step):
    return lax.rem(2 + 3 * step + 3 * lax.div(step, 2) + 2 * lax.div(step, 3), 4)


MIRROR = (0, 2, 1)


def kernel(
    b_hbm, h_hbm, d_hbm, p_hbm, gathered, fine, pro_off,
    hs, ht, ds, rhs, field, last, acc, pro_in,
    h_sem, d_sem, p_sem, b_sem,
    in_send, in_recv, halo_send, halo_recv, out_send, out_recv,
):
    g = lax.axis_index("group")
    o = lax.axis_index("owner")
    core = lax.rem(o, 2)
    times = (core, 1 - core)

    def slab(j):
        return lax.rem(g + offset_of(j), 4)

    def part(index):
        return pl.ds(pl.multiple_of(index * PART, PART), PART)

    d_load = pltpu.make_async_copy(d_hbm, ds, d_sem)
    d_load.start()
    b_load = pltpu.make_async_copy(b_hbm.at[:, :, 0, :, part(g), :], rhs.at[:, :, g], b_sem)
    b_load.start()

    def h_load(kind, j, z):
        t, y = times[kind], slab(j)
        return pltpu.make_async_copy(
            h_hbm.at[:, t, z, y], hs.at[:, t, z, y], h_sem.at[kind, j, z]
        )

    for kind in (OFF, IN):

        def start_loads(j, carry, kind=kind):
            for z in range(2):
                h_load(kind, j, z).start()
            return carry

        lax.fori_loop(0, 4, start_loads, 0)
    p_loads = [
        pltpu.make_async_copy(p_hbm.at[times[IN], :, 0], pro_in, p_sem.at[IN]),
        pltpu.make_async_copy(p_hbm.at[times[OFF], :, 0], pro_off, p_sem.at[OFF]),
    ]
    for load in p_loads:
        load.start()

    barrier = pltpu.get_barrier_semaphore()
    for k in (1, 2, 3):
        pl.semaphore_signal(
            barrier, inc=1, device_id={"group": lax.rem(g + k, 4)}, device_id_type=MESH
        )
    for k in (1, 31):
        pl.semaphore_signal(
            barrier, inc=1, device_id={"owner": lax.rem(o + k, 32)}, device_id_type=MESH
        )

    def in_copy(kind, j, arrives=False):
        peer, t = slab(j), times[kind]
        return pltpu.make_async_remote_copy(
            src_ref=b_hbm.at[t, :, 0, :, part(peer), :],
            dst_ref=rhs.at[t, :, peer if arrives else g],
            send_sem=in_send.at[kind, j],
            recv_sem=in_recv.at[kind, j if arrives else MIRROR[j]],
            device_id={"group": peer},
            device_id_type=MESH,
        )

    def halo_copy(kind, it, j, arrives=False):
        t, y = times[kind], slab(j)
        return pltpu.make_async_remote_copy(
            src_ref=field.at[it, t + 1, :, y],
            dst_ref=field.at[it, 3 * t if arrives else 3 - 3 * t, :, y],
            send_sem=halo_send.at[kind, it, j],
            recv_sem=halo_recv.at[kind, it, j],
            device_id={"owner": lax.rem(o + 31 + 2 * t, 32)},
            device_id_type=MESH,
        )

    sites = [(z, x) for z in range(2) for x in range(4)]

    def transpose_slab(kind, j):
        t, y = times[kind], slab(j)
        inner, outer = 6 + t, 7 - t
        for z in range(2):
            h_load(kind, j, z).wait()
            for x in range(4):
                blocks = [hs[k, t, z, y, x] for k in range(4)]
                blocks.append(hs[4, t, z, y, x] + hs[5, t, z, y, x])
                blocks.append(hs[inner, t, z, y, x])
                blocks.append(hs[outer, t, z, y, x])
                for k, block in enumerate(blocks):
                    ht[t, z, y, x, k * C : (k + 1) * C, :] = block.T

    def transpose_inverse(kind, j):
        t, y = times[kind], slab(j)
        for z, x in sites:
            ds[t, z, y, x] = ds[t, z, y, x].T

    def first(kind, j):
        t, y = times[kind], slab(j)
        for z, x in sites:
            field[0, t + 1, z, y, x] = dot(rhs[t, z, y, x], ds[t, z, y, x]).astype(BF16)
        halo_copy(kind, 0, j).start()

    def near(it, t, z, y, x):
        return [
            field[it, t + 1, z, y, (x + 1) % 4],
            field[it, t + 1, z, y, (x + 3) % 4],
            field[it, t + 1, z, lax.rem(y + 1, 4), x],
            field[it, t + 1, z, lax.rem(y + 3, 4), x],
            field[it, t + 1, 1 - z, y, x],
            field[it, 2 - t, z, y, x],
        ]

    def interior(it, pair):
        t = times[OFF]
        for j in (2 * pair, 2 * pair + 1):
            y = slab(j)
            for q, (z, x) in enumerate(sites):
                total = dot(
                    jnp.concatenate(near(it, t, z, y, x), axis=1), ht[t, z, y, x, : 6 * C, :]
                )
                acc[j, q] = rhs[t, z, y, x].astype(F32) - total

    def finish_off(it, j, store):
        t, y = times[OFF], slab(j)
        halo_copy(OFF, it, j, True).wait_recv()
        remainders = [
            acc[j, q] - dot(field[it, 3 * t, z, y, x], ht[t, z, y, x, 6 * C :, :])
            for q, (z, x) in enumerate(sites)
        ]
        for remainder, (z, x) in zip(remainders, sites):
            value = dot(remainder.astype(BF16), ds[t, z, y, x]).astype(BF16)
            store(t, z, y, x, value)

    def finish_in(it, steps, stores):
        t = times[IN]
        for j in steps:
            halo_copy(IN, it, j, True).wait_recv()
        places = [(k, slab(j), z, x) for k, j in enumerate(steps) for z, x in sites]
        remainders = [
            rhs[t, z, y, x].astype(F32)
            - dot(
                jnp.concatenate(near(it, t, z, y, x) + [field[it, 3 * t, z, y, x]], axis=1),
                ht[t, z, y, x],
            )
            for k, y, z, x in places
        ]
        for remainder, (k, y, z, x) in zip(remainders, places):
            value = dot(remainder.astype(BF16), ds[t, z, y, x]).astype(BF16)
            stores[k](t, z, y, x, value)

    def for_each(body, start=0, stop=4):
        def step(j, carry):
            body(j)
            return carry

        lax.fori_loop(start, stop, step, 0)

    def prepare_off(j):
        transpose_inverse(OFF, j)
        transpose_slab(OFF, j)

    d_load.wait()
    for_each(prepare_off, 0, 1)
    pl.semaphore_wait(barrier, 5)
    for kind in (OFF, IN):
        for j in range(3):
            in_copy(kind, j).start()
    for_each(prepare_off, 1, 4)
    b_load.wait()
    first(OFF, 3)
    for_each(lambda j: transpose_inverse(IN, j))
    for_each(lambda j: transpose_slab(IN, j), 0, 2)
    for j in range(3):
        in_copy(OFF, j, True).wait_recv()
        first(OFF, j)
    for_each(lambda j: transpose_slab(IN, j), 2, 4)
    first(IN, 3)
    for j in range(3):
        in_copy(IN, j, True).wait_recv()
        first(IN, j)

    for it in range(ITERS - 2):

        def store(t, z, y, x, value, it=it):
            field[it + 1, t + 1, z, y, x] = value

        def step_off(j, it=it, store=store):
            finish_off(it, j, store)
            halo_copy(OFF, it + 1, j).start()

        def step_in(pair, it=it, store=store):
            steps = (2 * pair, 2 * pair + 1)
            finish_in(it, steps, (store, store))
            for j in steps:
                halo_copy(IN, it + 1, j).start()

        for_each(lambda pair: interior(it, pair), 0, 2)
        if it == 0:
            for_each(lambda j: transpose_slab(IN, j), 4, 4)
        for_each(step_off)
        for_each(step_in, 0, 2)

    def out_copy(kind, j):
        peer, t = slab(j), times[kind]
        return pltpu.make_async_remote_copy(
            src_ref=last.at[t, :, peer],
            dst_ref=gathered.at[t, :, :, part(g), :],
            send_sem=out_send.at[kind, j],
            recv_sem=out_recv.at[kind, j],
            device_id={"group": peer},
            device_id_type=MESH,
        )

    def store_last(t, z, y, x, value):
        last[t, z, y, x] = value

    def store_own(t, z, y, x, value):
        gathered[t, z, x, part(g), :] = value

    it = ITERS - 2

    def last_off(j):
        finish_off(it, j, store_last)
        out_copy(OFF, j).start()

    for_each(lambda pair: interior(it, pair), 0, 2)
    finish_in(it, (0, 1), (store_last, store_last))
    for j in (0, 1):
        out_copy(IN, j).start()
    finish_in(it, (2, 3), (store_last, store_own))
    out_copy(IN, 2).start()
    for_each(last_off, 0, 3)
    finish_off(it, 3, store_own)

    for load in p_loads:
        load.wait()
    for j in range(3):
        out_copy(IN, j).wait_recv()
    for z, x in sites:
        fine[z, x] = dot(gathered[times[IN], z, x], pro_in[z, x]).astype(BF16)
    for j in range(3):
        out_copy(OFF, j).wait_recv()

    for kind in (OFF, IN):
        for j in range(3):
            in_copy(kind, j).wait_send()
            out_copy(kind, j).wait_send()
        for k in range(ITERS - 1):
            for_each(lambda j: halo_copy(kind, k, j).wait_send())


def write_kernel(coarse, fine, pro_off, c_hbm, f_hbm, fine_off, sem):
    core = lax.rem(lax.axis_index("owner"), 2)
    copies = [
        pltpu.make_async_copy(coarse, c_hbm.at[:, :, 0], sem.at[0]),
        pltpu.make_async_copy(fine, f_hbm.at[1 - core, :, 0], sem.at[1]),
    ]
    for copy in copies:
        copy.start()
    for z in range(2):
        for x in range(4):
            fine_off[z, x] = dot(coarse[core, z, x], pro_off[z, x]).astype(BF16)
        copy = pltpu.make_async_copy(fine_off.at[z], f_hbm.at[core, z, 0], sem.at[2 + z])
        copy.start()
        copies.append(copy)
    for copy in copies:
        copy.wait()


def on_device(right_side, hops, diag_inverse, prolongator):
    vmem, dma = pltpu.VMEM, pltpu.SemaphoreType.DMA
    width = prolongator.shape[-1]
    parts = pl.pallas_call(
        kernel,
        out_shape=(
            vmem((2, 2, 4, C, C), BF16),
            vmem((2, 4, C, width), BF16),
            vmem((2, 4, C, width), BF16),
        ),
        in_specs=[pl.BlockSpec(memory_space=pl.ANY)] * 4,
        out_specs=(pl.BlockSpec(memory_space=vmem),) * 3,
        scratch_shapes=[
            vmem((8, 2, 2, 4, 4, C, C), BF16),
            vmem((2, 2, 4, 4, DIRS * C, C), BF16),
            vmem((2, 2, 4, 4, C, C), BF16),
            vmem((2, 2, 4, 4, PART, C), BF16),
            vmem((ITERS - 1, 4, 2, 4, 4, PART, C), BF16),
            vmem((2, 2, 4, 4, PART, C), BF16),
            vmem((4, 8, PART, C), F32),
            vmem((2, 4, C, width), BF16),
            dma((2, 4, 2)),
            dma,
            dma((2,)),
            dma,
            dma((2, 3)),
            dma((2, 3)),
            dma((2, ITERS - 1, 4)),
            dma((2, ITERS - 1, 4)),
            dma((2, 3)),
            dma((2, 3)),
        ],
        compiler_params=pltpu.CompilerParams(
            collective_id=0, has_side_effects=True, vmem_limit_bytes=VMEM_LIMIT
        ),
        cost_estimate=pl.CostEstimate(
            flops=2 * 64 * 28 * C * C * PART, bytes_accessed=24 * 1024 * 1024, transcendentals=0
        ),
    )(right_side, hops, diag_inverse, prolongator)
    return pl.pallas_call(
        write_kernel,
        out_shape=(
            jax.ShapeDtypeStruct(right_side.shape, BF16),
            jax.ShapeDtypeStruct(prolongator.shape, BF16),
        ),
        in_specs=[pl.BlockSpec(memory_space=vmem)] * 3,
        out_specs=(pl.BlockSpec(memory_space=pl.ANY),) * 2,
        scratch_shapes=[vmem((2, 4, C, width), BF16), dma((4,))],
    )(*(pltpu.with_memory_space_constraint(array, vmem) for array in parts))


def solution(mesh):
    placed = (
        P("owner", None, "group", None, None, None),
        P(None, "owner", None, None, None, None, None),
        P("owner", None, None, None, None, None),
        P("owner", None, "group", None, None, None),
    )
    return jax.shard_map(
        on_device,
        mesh=mesh,
        in_specs=placed,
        out_specs=(
            P("owner", None, "group", None, None, None),
            P("owner", None, "group", None, None, None),
        ),
        check_vma=False,
    )
```

time: 221 us -> 37.5 us (0.17); the launches traced: 217 us -> 37.3 us
  matrix products: 144 us -> 0 us
  Pallas kernels: 0 us -> 36.7 us
  waiting for transfers between devices: 35.8 us -> 0 us
  starting transfers between devices: 15.7 us -> 0 us
  between operations: 14.6 us -> 0.64 us
  local copies, waits for them, and re-layouts: 6.74 us -> 0 us
    dot_general x29 -> x0, matrix products: 144 us -> none  [the longest x24 129 us: hop_total(): jnp.einsum('tzyxrd,tzyxcd->tzyxrc', neighbour, hops[direction], preferred...]
    pallas_call x0 -> x2, Pallas kernels: none -> 36.7 us  [the longest x1 35.4 us: on_device(): pl.pallas_call(kernel, out_shape=(vmem((2, 2, 4, C, C), BF16), vmem((2, 4...]
    all_gather x1 -> x0, waiting for transfers between devices: 35.1 us -> none  [on_device(): gathered = lax.all_gather(right_side, 'group', axis=2, tiled=True)]
    ppermute x6 -> x0, starting transfers between devices: 15.6 us -> none  [the longest x3 14.8 us: with_halo(): lax.ppermute(head, axis, [((i + 1) % count, i) for i in range(count)])]
    slice x18 -> x0, local copies, waits for them, and re-layouts: 6.61 us -> none  [the longest x6 2.87 us: on_device(): jnp.roll(iterate, 1, 3)]
  transfers between devices with their start and end apart: 7 -> 0, of which waited for: 1 -> 0; matrix products, arithmetic and copies ran while one was open for 26% -> 0% of each run, Pallas kernels for 0% -> 0%
where the time goes in v2:
time: 37.5 us; the launch traced here: 37.3 us
  Pallas kernels  36.7 us (98%)
  between operations  0.64 us (2%)
    pallas_call x1, Pallas kernels, on_device(): pl.pallas_call(kernel, out_shape=(vmem((2, 2, 4, C, C), BF16), vmem((2, 4...  35.4 us
    pallas_call x1, Pallas kernels, on_device(): pl.pallas_call(write_kernel, out_shape=(jax.ShapeDtypeStruct(right_side.s...  1.35 us

profile of v2, /device:TPU:0, one launch (start us, length us, event | category | flops | bytes accessed | tf_op | source)
XLA Modules:
  0.0 37.3 jit_solution(18012254121517432549)
XLA Ops:
  0.6 35.4 %shard_map.59 = (bf16[2,2,4,128,128]{4,3,2,1,0:T(8,128)(2,1)S(1)}, bf16[2,4,128,384]{3,2,1,0:T(8,128)(2,1)S(1)}, bf16[2,4,128,384]{3,2,1,0:T(8,128)(2,1)S(1)}) custom-call(bf16[2,2,1,4,128,128]{5,4,3,2,1,0:T(8,128)(2,1)} %b_hbm.1, bf16[8,2,2,4,4,128,128]{6,5,4,3,2,1,0:T(8,128)(2,1)} %h_hbm.1, bf16[2,2,4,4,128,128]{5,4,3,2,1,0:T(8,128)(2,1)} %d_hbm.1, ...), custom_call_target="tpu_custom_call" | custom-call | flops 1879048192 | bytes 25165824 | tf_op jit(solution)/shard_map/pallas_call | solution.py:305
  36.0 1.4 %shard_map.60 = (bf16[2,2,1,4,128,128]{5,4,3,2,1,0:T(8,128)(2,1)}, bf16[2,2,1,4,128,384]{5,4,3,2,1,0:T(8,128)(2,1)}) custom-call(bf16[2,2,4,128,128]{4,3,2,1,0:T(8,128)(2,1)S(1)} %get-tuple-element.5.coarse, bf16[2,4,128,384]{3,2,1,0:T(8,128)(2,1)S(1)} %get-tuple-element.6.fine, bf16[2,4,128,384]{3,2,1,0:T(8,128)(2,1)S(1)} %get-tuple-element.7.pro_off), custom_call_target="tpu_custom_call" | custom-call | tf_op jit(solution)/shard_map/pallas_call | solution.py:341

commit v3 on v2

--- a/solution.py
+++ b/solution.py
@@ -48,6 +48,16 @@
     def part(index):
         return pl.ds(pl.multiple_of(index * PART, PART), PART)
 
+    barrier = pltpu.get_barrier_semaphore()
+    for k in (1, 31):
+        pl.semaphore_signal(
+            barrier, inc=1, device_id={"owner": lax.rem(o + k, 32)}, device_id_type=MESH
+        )
+    for k in (1, 2, 3):
+        pl.semaphore_signal(
+            barrier, inc=1, device_id={"group": lax.rem(g + k, 4)}, device_id_type=MESH
+        )
+
     d_load = pltpu.make_async_copy(d_hbm, ds, d_sem)
     d_load.start()
     b_load = pltpu.make_async_copy(b_hbm.at[:, :, 0, :, part(g), :], rhs.at[:, :, g], b_sem)
@@ -73,16 +83,6 @@
     ]
     for load in p_loads:
         load.start()
-
-    barrier = pltpu.get_barrier_semaphore()
-    for k in (1, 2, 3):
-        pl.semaphore_signal(
-            barrier, inc=1, device_id={"group": lax.rem(g + k, 4)}, device_id_type=MESH
-        )
-    for k in (1, 31):
-        pl.semaphore_signal(
-            barrier, inc=1, device_id={"owner": lax.rem(o + k, 32)}, device_id_type=MESH
-        )
 
     def in_copy(kind, j, arrives=False):
         peer, t = slab(j), times[kind]
@@ -194,10 +194,12 @@
     d_load.wait()
     for_each(prepare_off, 0, 1)
     pl.semaphore_wait(barrier, 5)
-    for kind in (OFF, IN):
-        for j in range(3):
-            in_copy(kind, j).start()
-    for_each(prepare_off, 1, 4)
+    for j in range(3):
+        in_copy(OFF, j).start()
+    for_each(prepare_off, 1, 3)
+    for j in range(3):
+        in_copy(IN, j).start()
+    for_each(prepare_off, 3, 4)
     b_load.wait()
     first(OFF, 3)
     for_each(lambda j: transpose_inverse(IN, j))
@@ -270,15 +272,17 @@
         out_copy(IN, j).wait_recv()
     for z, x in sites:
         fine[z, x] = dot(gathered[times[IN], z, x], pro_in[z, x]).astype(BF16)
-    for j in range(3):
-        out_copy(OFF, j).wait_recv()
-
     for kind in (OFF, IN):
         for j in range(3):
             in_copy(kind, j).wait_send()
-            out_copy(kind, j).wait_send()
         for k in range(ITERS - 1):
             for_each(lambda j: halo_copy(kind, k, j).wait_send())
+    for j in range(3):
+        out_copy(IN, j).wait_send()
+    for j in range(3):
+        out_copy(OFF, j).wait_send()
+    for j in range(3):
+        out_copy(OFF, j).wait_recv()
 
 
 def write_kernel(coarse, fine, pro_off, c_hbm, f_hbm, fine_off, sem):

time: 37.5 us -> 37.1 us (0.989)
  no operation moved by 1% of the time
where the time goes in v3:
time: 37.1 us; the launch traced here: 37 us
  Pallas kernels  36.4 us (98%)
  between operations  0.64 us (2%)
    pallas_call x1, Pallas kernels, on_device(): pl.pallas_call(kernel, out_shape=(vmem((2, 2, 4, C, C), BF16), vmem((2, 4...  35 us
    pallas_call x1, Pallas kernels, on_device(): pl.pallas_call(write_kernel, out_shape=(jax.ShapeDtypeStruct(right_side.s...  1.35 us

profile of v3, /device:TPU:0, one launch (start us, length us, event | category | flops | bytes accessed | tf_op | source)
XLA Modules:
  0.0 37.0 jit_solution(17042525317054929879)
XLA Ops:
  0.6 35.0 %shard_map.59 = (bf16[2,2,4,128,128]{4,3,2,1,0:T(8,128)(2,1)S(1)}, bf16[2,4,128,384]{3,2,1,0:T(8,128)(2,1)S(1)}, bf16[2,4,128,384]{3,2,1,0:T(8,128)(2,1)S(1)}) custom-call(bf16[2,2,1,4,128,128]{5,4,3,2,1,0:T(8,128)(2,1)} %b_hbm.1, bf16[8,2,2,4,4,128,128]{6,5,4,3,2,1,0:T(8,128)(2,1)} %h_hbm.1, bf16[2,2,4,4,128,128]{5,4,3,2,1,0:T(8,128)(2,1)} %d_hbm.1, ...), custom_call_target="tpu_custom_call" | custom-call | flops 1879048192 | bytes 25165824 | tf_op jit(solution)/shard_map/pallas_call | solution.py:309
  35.7 1.4 %shard_map.60 = (bf16[2,2,1,4,128,128]{5,4,3,2,1,0:T(8,128)(2,1)}, bf16[2,2,1,4,128,384]{5,4,3,2,1,0:T(8,128)(2,1)}) custom-call(bf16[2,2,4,128,128]{4,3,2,1,0:T(8,128)(2,1)S(1)} %get-tuple-element.5.coarse, bf16[2,4,128,384]{3,2,1,0:T(8,128)(2,1)S(1)} %get-tuple-element.6.fine, bf16[2,4,128,384]{3,2,1,0:T(8,128)(2,1)S(1)} %get-tuple-element.7.pro_off), custom_call_target="tpu_custom_call" | custom-call | tf_op jit(solution)/shard_map/pallas_call | solution.py:345

commit v4 on v3

--- a/solution.py
+++ b/solution.py
@@ -229,10 +229,8 @@
                 halo_copy(IN, it + 1, j).start()
 
         for_each(lambda pair: interior(it, pair), 0, 2)
-        if it == 0:
-            for_each(lambda j: transpose_slab(IN, j), 4, 4)
+        for_each(step_in, 0, 2)
         for_each(step_off)
-        for_each(step_in, 0, 2)
 
     def out_copy(kind, j):
         peer, t = slab(j), times[kind]
@@ -296,9 +294,13 @@
     for z in range(2):
         for x in range(4):
             fine_off[z, x] = dot(coarse[core, z, x], pro_off[z, x]).astype(BF16)
-        copy = pltpu.make_async_copy(fine_off.at[z], f_hbm.at[core, z, 0], sem.at[2 + z])
-        copy.start()
-        copies.append(copy)
+            if x % 2:
+                pair = pl.ds(x - 1, 2)
+                copy = pltpu.make_async_copy(
+                    fine_off.at[z, pair], f_hbm.at[core, z, 0, pair], sem.at[2 + 2 * z + x // 2]
+                )
+                copy.start()
+                copies.append(copy)
     for copy in copies:
         copy.wait()
 
@@ -350,7 +352,7 @@
         ),
         in_specs=[pl.BlockSpec(memory_space=vmem)] * 3,
         out_specs=(pl.BlockSpec(memory_space=pl.ANY),) * 2,
-        scratch_shapes=[vmem((2, 4, C, width), BF16), dma((4,))],
+        scratch_shapes=[vmem((2, 4, C, width), BF16), dma((6,))],
     )(*(pltpu.with_memory_space_constraint(array, vmem) for array in parts))
 
 

time: 37.1 us -> 36.4 us (0.981)
  Pallas kernels: 36.4 us -> 35.6 us
    pallas_call x1, Pallas kernels: 35 us -> 34.3 us  [on_device(): pl.pallas_call(kernel, out_shape=(vmem((2, 2, 4, C, C), BF16), vmem((2, 4...]
where the time goes in v4:
time: 36.4 us; the launch traced here: 36.3 us
  Pallas kernels  35.6 us (98%)
  between operations  0.64 us (2%)
    pallas_call x1, Pallas kernels, on_device(): pl.pallas_call(kernel, out_shape=(vmem((2, 2, 4, C, C), BF16), vmem((2, 4...  34.3 us
    pallas_call x1, Pallas kernels, on_device(): pl.pallas_call(write_kernel, out_shape=(jax.ShapeDtypeStruct(right_side.s...  1.37 us

profile of v4, /device:TPU:0, one launch (start us, length us, event | category | flops | bytes accessed | tf_op | source)
XLA Modules:
  0.0 36.3 jit_solution(10107431084550069308)
XLA Ops:
  0.6 34.3 %shard_map.59 = (bf16[2,2,4,128,128]{4,3,2,1,0:T(8,128)(2,1)S(1)}, bf16[2,4,128,384]{3,2,1,0:T(8,128)(2,1)S(1)}, bf16[2,4,128,384]{3,2,1,0:T(8,128)(2,1)S(1)}) custom-call(bf16[2,2,1,4,128,128]{5,4,3,2,1,0:T(8,128)(2,1)} %b_hbm.1, bf16[8,2,2,4,4,128,128]{6,5,4,3,2,1,0:T(8,128)(2,1)} %h_hbm.1, bf16[2,2,4,4,128,128]{5,4,3,2,1,0:T(8,128)(2,1)} %d_hbm.1, ...), custom_call_target="tpu_custom_call" | custom-call | flops 1879048192 | bytes 25165824 | tf_op jit(solution)/shard_map/pallas_call | solution.py:311
  34.9 1.4 %shard_map.60 = (bf16[2,2,1,4,128,128]{5,4,3,2,1,0:T(8,128)(2,1)}, bf16[2,2,1,4,128,384]{5,4,3,2,1,0:T(8,128)(2,1)}) custom-call(bf16[2,2,4,128,128]{4,3,2,1,0:T(8,128)(2,1)S(1)} %get-tuple-element.5.coarse, bf16[2,4,128,384]{3,2,1,0:T(8,128)(2,1)S(1)} %get-tuple-element.6.fine, bf16[2,4,128,384]{3,2,1,0:T(8,128)(2,1)S(1)} %get-tuple-element.7.pro_off), custom_call_target="tpu_custom_call" | custom-call | tf_op jit(solution)/shard_map/pallas_call | solution.py:347
